TPU v7x, 128 devices: a whole 4x4x4 slice. The times are simulated.
128 devices in a mesh: replica: 8 (over y_lo, x), fsdp: 16 (over z, y_hi, core).
Axes of the slice: x: 4, y: 4 (y_hi: 2, y_lo: 2; y = y_hi * 2 + y_lo), z: 4, core: 2. Of those that a mesh axis runs over, the one named last changes fastest.
Arguments:
- pseudo_grads: bfloat16 [8, 8192, 8192], P('replica', None, 'fsdp'), may hold values from -6 to 6
- exponents: int32 [8, 8192, 64], P('replica', None, 'fsdp'), may hold values from -6 to 1
- master: float32 [8192, 8192], P(('replica', 'fsdp')), may hold values from -6 to 6
- momentum: float32 [8192, 8192], P(('replica', 'fsdp')), may hold values from -4 to 4
- layout: int32 [8], replicated, may hold values from 0 to 7, each once
Outputs:
- new_master: float32 [8192, 8192], P(('replica', 'fsdp'))
- new_momentum: float32 [8192, 8192], P(('replica', 'fsdp'))
- island_params: bfloat16 [8192, 8192], P(None, 'fsdp')
Inputs may be any that keep to these rules, and one draw needn't show every extreme that they name: `layout`: a permutation of the layers.
All inputs are finite; a program needn't handle non-finite values.
Results may differ from a plain program's by a relative error of at most 0.0095.
Values may be sent and summed in bfloat16 or wider, within the bound.
A program may use at most 192 MiB of HBM per device.

v0:
```python
import jax
import jax.numpy as jnp
from jax import lax
from jax.sharding import PartitionSpec as P

outer_rate = 0.7
outer_momentum = 0.9


def block_scale(exponents):
    scale = jnp.zeros(exponents.shape, jnp.float32)
    for level in range(-6, 2):
        scale = jnp.where(exponents == level, jnp.float32(2.0**level), scale)
    return scale


def decode(coded, exponents):
    shape = coded.shape
    blocks = coded.reshape(shape[:-1] + (shape[-1] // 128, 128)).astype(jnp.float32)
    return (blocks * block_scale(exponents)[..., None]).reshape(shape)


def per_device(pseudo_grads, exponents, master, momentum, layout):
    replicas = lax.axis_size("replica")
    coded = pseudo_grads[0]
    coded_exp = exponents[0]
    partial_sum = lax.psum_scatter(
        decode(coded, coded_exp).astype(jnp.bfloat16), "replica", scatter_dimension=0, tiled=True
    ).astype(jnp.float32)
    total = lax.all_to_all(partial_sum, "fsdp", split_axis=0, concat_axis=1, tiled=True)
    average = total / jnp.float32(replicas)
    new_momentum = outer_momentum * momentum + average
    new_master = master - outer_rate * (average + outer_momentum * new_momentum)
    rounded = new_master.astype(jnp.bfloat16)
    local_rows = lax.all_to_all(rounded, "fsdp", split_axis=1, concat_axis=0, tiled=True)
    island = lax.all_gather(local_rows, "replica", axis=0, tiled=True)
    layer_count = layout.shape[0]
    grouped = island.reshape(layer_count, island.shape[0] // layer_count, island.shape[1])
    island_params = jnp.take(grouped, layout, axis=0).reshape(island.shape)
    return (new_master, new_momentum, island_params)


def solution(mesh):
    placed = (
        P("replica", None, "fsdp"),
        P("replica", None, "fsdp"),
        P(("replica", "fsdp"), None),
        P(("replica", "fsdp"), None),
        P(),
    )
    return jax.shard_map(
        per_device,
        mesh=mesh,
        in_specs=placed,
        out_specs=(P(("replica", "fsdp"), None), P(("replica", "fsdp"), None), P(None, "fsdp")),
        check_vma=False,
    )
```

profile of v0, /device:TPU:0, one launch (start us, length us, event | category | flops | bytes accessed | tf_op | source)
XLA Modules:
  0.0 304.0 jit_solution(11877854920995589829)
XLA Ops:
  7.2 0.0 reduce-scatter.2.cloned.1.call-start
  7.2 1.0 select_bitcast_fusion
  8.3 2.7 copy.17
  10.9 15.9 %mul.23 = f32[8192,4,128]{2,1,0:T(4,128)S(1)} broadcast(f32[8192,4]{1,0:T(8,128)} %copy.17), dimensions={0,1} | broadcast | bytes 16908288 | tf_op jit(solution)/shard_map/mul | solution.py:20
  26.8 9.3 %fusion = bf16[8192,512]{1,0:T(8,128)(2,1)} fusion(f32[1024,8,4,128]{3,2,1,0:T(4,128)S(1)} %bitcast.31, bf16[1,8192,512]{2,1,0:T(8,128)(2,1)} %param.5), kind=kLoop, calls=%fused_computation.2 | loop fusion | flops 12582912 | bytes 33554432 | tf_op jit(solution)/shard_map/convert_element_type | solution.py:28
  36.1 0.0 reduce-scatter.2.cloned.1.call-update
  36.1 0.0 all-gather.2.cloned.1.call-start
  36.2 95.2 %reduce-scatter.2.cloned.1.call-done = bf16[1024,512]{1,0:T(8,128)(2,1)} async-done(((bf16[8192,512]{1,0:T(8,128)(2,1)}), bf16[1024,512]{1,0:T(8,128)(2,1)}) %reduce-scatter.2.cloned.1.call-update) | async-done | bytes 1048592 | tf_op jit(solution)/shard_map/reduce_scatter | solution.py:27
  131.4 1.5 convert.3
  132.9 35.7 %all_to_all.36 = f32[16,64,512]{2,1,0:T(8,128)S(1)} all-to-all(f32[16,64,512]{2,1,0:T(8,128)S(1)} %convert.3), channel_id=1, replica_groups=mesh['replica'=8,'fsdp'=16] {'fsdp'}, dimensions={0} | all-to-all | bytes 4194304 | tf_op jit(solution)/shard_map/all_to_all | solution.py:30
  168.6 0.3 multiply_bitcast_fusion
  168.9 0.0 copy-start
  168.9 0.0 copy-start.1
  168.9 0.2 copy.21
  169.1 1.4 copy-done
  170.5 0.6 copy-done.1
  171.1 2.6 fusion.1
  173.7 0.1 copy.27
  173.8 0.0 copy-start.2
  173.8 21.3 %all_to_all.37 = bf16[64,16,512]{2,0,1:T(8,128)(2,1)} all-to-all(bf16[64,16,512]{2,0,1:T(8,128)(2,1)S(1)} %bitcast.35), channel_id=1, replica_groups=mesh['replica'=8,'fsdp'=16] {'fsdp'}, dimensions={1} | all-to-all | bytes 2097152 | tf_op jit(solution)/shard_map/all_to_all | solution.py:35
  195.1 0.0 all-gather.2.cloned.1.call-update
  195.1 0.0 copy-done.2
  195.1 0.1 broadcast_bitcast_fusion
  195.2 86.4 %all-gather.2.cloned.1.call-done = bf16[8192,512]{1,0:T(8,128)(2,1)} async-done(((bf16[1024,512]{1,0:T(8,128)(2,1)}), bf16[8192,512]{1,0:T(8,128)(2,1)}) %all-gather.2.cloned.1.call-update) | async-done | bytes 8388624 | tf_op jit(solution)/shard_map/all_gather | solution.py:36
  281.6 8.1 %gather_fusion = bf16[8,1024,512]{2,1,0:T(8,128)(2,1)} fusion(bf16[8,1024,512]{2,1,0:T(8,128)(2,1)} %bitcast.32, s32[1024]{0:T(1024)S(1)} %pad_clamp_fusion), kind=kCustom, calls=%fused_computation | custom fusion | bytes 16777248 | tf_op jit(solution)/shard_map/jit(_take)/gather | solution.py:39
  289.7 7.5 %bitcast_select_fusion = bf16[8192,512]{1,0:T(8,128)(2,1)} fusion(bf16[8,1024,512]{2,1,0:T(8,128)(2,1)} %gather_fusion, pred[8192]{0:T(1024)(128)(4,1)S(1)} %bitcast.38), kind=kLoop, calls=%fused_computation.3 | loop fusion | flops 4194304 | bytes 16785408 | tf_op jit(solution)/shard_map/jit(_take)/select_n | solution.py:39
  (4 shorter events, 0.0 us)
Async XLA Ops:
  7.2 124.2 %reduce-scatter.2.cloned.1.call-start = ((), (), s32[]{:S(2)}) async-start(), calls=%async_computation.3 | async-start | bytes 9437184 | tf_op jit(solution)/shard_map/reduce_scatter | solution.py:27
  36.1 245.5 %all-gather.2.cloned.1.call-start = ((), (), s32[]{:S(2)}) async-start(), calls=%async_computation.4 | async-start | bytes 9437184 | tf_op jit(solution)/shard_map/all_gather | solution.py:36
  168.9 1.6 copy-start
  168.9 2.2 copy-start.1
  173.8 21.3 %copy-start.2 = (s32[8]{0:T(128)S(1)}, s32[8]{0:T(128)}, u32[]{:S(2)}) copy-start(s32[8]{0:T(128)} %param.9) | copy-start | bytes 100
Sparse Core Ops, SparseCore 0:
  36.3 95.0 reduce-scatter.1
  195.2 86.3 all-gather.1
where the time goes:
time: 305 us; the launch traced here: 304 us
  waiting for transfers between devices  182 us (60%)
  blocking collectives  57 us (19%)
  local copies, waits for them, and re-layouts  29 us (10%)
  other arithmetic  22.1 us (7%)
  between operations  14.1 us (5%)
    reduce_scatter x1, waiting for transfers between devices, per_device(): lax.psum_scatter(decode(coded, coded_exp).astype(jnp.bfloat16), 'replica'...  95.2 us
    all_gather x1, waiting for transfers between devices, per_device(): island = lax.all_gather(local_rows, 'replica', axis=0, tiled=True)  86.4 us
    all_to_all x1, blocking collectives, per_device(): lax.all_to_all(partial_sum, 'fsdp', split_axis=0, concat_axis=1, tiled=True)  35.7 us
    all_to_all x1, blocking collectives, per_device(): lax.all_to_all(rounded, 'fsdp', split_axis=1, concat_axis=0, tiled=True)  21.3 us
    mul x1, local copies, waits for them, and re-layouts, decode(): return (blocks * block_scale(exponents)[..., None]).reshape(shape)  15.9 us
    convert_element_type x1, other arithmetic, per_device(): decode(coded, coded_exp).astype(jnp.bfloat16)  9.28 us
    gather x1, local copies, waits for them, and re-layouts, per_device(): island_params = jnp.take(grouped, layout, axis=0).reshape(island.shape)  8.06 us
    select_n x2, other arithmetic, per_device(): island_params = jnp.take(grouped, layout, axis=0).reshape(island.shape)  7.47 us
  transfers between devices with their start and end apart: 2, of which 2 were waited for; matrix products, arithmetic and copies ran while one was open for 0% of the time, Pallas kernels for 0%

commit v1 on v0

v1 whole, which is shorter than its diff:
```python
import jax
import jax.numpy as jnp
from jax import lax
from jax.experimental import pallas as pl
from jax.experimental.pallas import tpu as pltpu
from jax.sharding import PartitionSpec as P

MESH = pl.DeviceIdType.MESH
F32, BF16 = jnp.float32, jnp.bfloat16

outer_rate = 0.7
outer_momentum = 0.9

UNITS = 16
TILES = 16
XT = 9
XP = 5
YT = TILES - XT
YP = 3
YM = XT + YP


def bit(v, b):
    return (v // (1 << b)) % 2


def flip(a, b):
    return a + b - 2 * a * b


def xor16(f, t):
    return sum(flip(bit(f, b), bit(t, b)) * (1 << b) for b in range(4))


def block_scale(exponents):
    scale = jnp.zeros(exponents.shape, F32)
    for level in range(-6, 2):
        scale = jnp.where(exponents == level, F32(2.0**level), scale)
    return scale


def step_kernel(
    g, expt, master, momentum,
    isl, new_master, new_momentum,
    graw, dec, r1p, r1m, r1y, r2p, r2m, q2p, q2m, r3x, q3p, q3m, a2a, ret, mas, mom, omas, omom,
    g_sem, m_sem, o_sem, own_sem, rs_send, rs_recv, a_send, a_recv, b_send, b_recv, ag_send, ag_recv,
):
    rep, fs = lax.axis_index("replica"), lax.axis_index("fsdp")
    x, yl = rep % 4, rep // 4
    xp, xm, xo = (x + 1) % 4, (x + 3) % 4, (x + 2) % 4
    right, left, side = (yl * 4 + xp, fs), (yl * 4 + xm, fs), ((1 - yl) * 4 + x, fs)

    def own(t):
        return flip(yl, bit(t, 1))

    def partner(t):
        return (own(t) * 4 + x, xor16(fs, t))

    def columns(t):
        return pl.ds(pl.multiple_of(xor16(fs, t) * 512, 512), 512)

    def load_g(p):
        return pltpu.make_async_copy(g.at[:, xor16(fs, 2 * p) // 2], graw.at[p], g_sem.at[p])

    def load_m(t):
        return (
            pltpu.make_async_copy(master.at[:, columns(t)], mas.at[t], m_sem.at[0, t]),
            pltpu.make_async_copy(momentum.at[:, columns(t)], mom.at[t], m_sem.at[1, t]),
        )

    def store_m(t):
        return (
            pltpu.make_async_copy(omas.at[t], new_master.at[:, columns(t)], o_sem.at[0, t]),
            pltpu.make_async_copy(omom.at[t], new_momentum.at[:, columns(t)], o_sem.at[1, t]),
        )

    def remote(src, dst, send, recv, device):
        return pltpu.make_async_remote_copy(
            src_ref=src, dst_ref=dst, send_sem=send, recv_sem=recv, device_id=device, device_id_type=MESH
        )

    def rs(t, i):
        o = own(t)
        every = slice(None)
        src, dst, device = (
            (dec.at[t, every, xo, pl.ds(0, XP)], r1p, right),
            (dec.at[t, every, xo, pl.ds(XP, XT - XP)], r1m, left),
            (dec.at[t, 1 - o, every, pl.ds(XT, YT)], r1y, side),
            (dec.at[t, every, xp, pl.ds(0, XT)], r2p, right),
            (dec.at[t, every, xm, pl.ds(0, XT)], r2m, left),
            (dec.at[t, o, xo, pl.ds(XT, YP)], q2p, right),
            (dec.at[t, o, xo, pl.ds(YM, YT - YP)], q2m, left),
            (dec.at[t, 1 - o, x, pl.ds(0, XT)], r3x, side),
            (dec.at[t, o, xp, pl.ds(XT, YT)], q3p, right),
            (dec.at[t, o, xm, pl.ds(XT, YT)], q3m, left),
        )[i]
        return remote(src, dst.at[t], rs_send.at[t, i], rs_recv.at[t, i], device)

    def ag(t, i, arriving=False):
        o, j = own(t), xor16(fs, t)
        every = slice(None)
        cp, cm = (xm, xp) if arriving else (x, x)
        fp, fm = (xo, xo) if arriving else (xm, xp)
        mine = 1 - o if arriving else o
        ref, device = (
            (isl.at[j, mine, x, pl.ds(0, XT)], side),
            (isl.at[j, o, cp, pl.ds(XT, YT)], right),
            (isl.at[j, o, cm, pl.ds(XT, YT)], left),
            (isl.at[j, every, cp, pl.ds(0, XT)], right),
            (isl.at[j, every, cm, pl.ds(0, XT)], left),
            (isl.at[j, o, fp, pl.ds(XT, YP)], right),
            (isl.at[j, o, fm, pl.ds(YM, YT - YP)], left),
            (isl.at[j, every, fp, pl.ds(0, XP)], right),
            (isl.at[j, every, fm, pl.ds(XP, XT - XP)], left),
            (isl.at[j, mine, every, pl.ds(XT, YT)], side),
        )[i]
        return remote(ref, ref, ag_send.at[t, i], ag_recv.at[t, i], device)

    def go(t):
        return remote(dec.at[t, own(t), x], a2a.at[t], a_send.at[t], a_recv.at[t], partner(t))

    def back(t, arriving=False):
        place = isl.at[xor16(fs, t), own(t), x] if arriving else isl.at[fs, yl, x]
        return remote(ret.at[t], place, b_send.at[t], b_recv.at[t], partner(t))

    def back_own():
        return pltpu.make_async_copy(ret.at[0], isl.at[fs, yl, x], own_sem)

    def wide(ref, *at):
        return ref[at].astype(F32)

    lane_block = lax.broadcasted_iota(jnp.int32, (8, 512), 1) // 128
    pick = (lane_block == lax.broadcasted_iota(jnp.int32, (8, 512), 0)).astype(F32)

    def decode(p):
        load_g(p).wait()
        base = xor16(fs, 2 * p) // 2 * 128
        odd = fs % 2

        def one(l, _):
            rows = pl.ds(pl.multiple_of(l * 1024 + base, 128), 128)
            scale = block_scale(expt[:, rows])
            scale = jnp.concatenate([scale, jnp.zeros((4, 128), F32)], axis=0)
            spread = lax.dot_general(scale, pick, (((0,), (0,)), ((), ())), preferred_element_type=F32)
            for k in range(4):
                cols = pl.ds(k * 128, 128)
                piece = (graw[p, l, :, cols].astype(F32) * spread[:, k * 128 : (k + 1) * 128]).astype(BF16)
                piece = piece.reshape(2, 4, 16, 128)
                for h in range(2):
                    dec[2 * p + flip(odd, h), l // 4, l % 4, pl.ds(4 * k, 4)] = piece[h]
            return 0

        lax.fori_loop(0, 8, one, 0)

    def first(t):
        for i in range(3):
            rs(t, i).start()

    def second(t):
        o = own(t)
        for i in range(3):
            rs(t, i).wait_recv()
        at = (t, slice(None), xp, pl.ds(0, XP))
        dec[at] = (wide(dec, *at) + wide(r1p, t)).astype(BF16)
        rs(t, 3).start()
        at = (t, slice(None), xm, pl.ds(XP, XT - XP))
        dec[at] = (wide(dec, *at) + wide(r1m, t)).astype(BF16)
        rs(t, 4).start()
        at = (t, o, slice(None), pl.ds(XT, YT))
        dec[at] = (wide(dec, *at) + wide(r1y, t)).astype(BF16)
        rs(t, 5).start()
        rs(t, 6).start()
        for i in range(3):
            rs(t, i).wait_send()

    def third(t):
        o = own(t)
        for i in range(3, 7):
            rs(t, i).wait_recv()
        at = (t, 1 - o, x, pl.ds(0, XT))
        dec[at] = (wide(dec, *at) + wide(r2p, t, 1 - o) + wide(r2m, t, 1 - o)).astype(BF16)
        rs(t, 7).start()
        at = (t, o, xp, pl.ds(XT, YP))
        dec[at] = (wide(dec, *at) + wide(q2p, t)).astype(BF16)
        rs(t, 8).start()
        at = (t, o, xm, pl.ds(YM, YT - YP))
        dec[at] = (wide(dec, *at) + wide(q2m, t)).astype(BF16)
        rs(t, 9).start()
        for i in range(3, 7):
            rs(t, i).wait_send()

    def fourth(t):
        o = own(t)
        for i in range(7, 10):
            rs(t, i).wait_recv()
        at = (t, o, x, pl.ds(0, XT))
        dec[at] = (wide(dec, *at) + wide(r2p, t, o) + wide(r2m, t, o) + wide(r3x, t)).astype(BF16)
        at = (t, o, x, pl.ds(XT, YT))
        dec[at] = (wide(dec, *at) + wide(q3p, t) + wide(q3m, t)).astype(BF16)

        @pl.when(t > 0)
        def _():
            go(t).start()

        @pl.when(t == 0)
        def _():
            a2a[0] = dec[0, yl, x]

        for i in range(7, 10):
            rs(t, i).wait_send()

    def fifth(t):
        for copy in load_m(t):
            copy.wait()

        @pl.when(t > 0)
        def _():
            go(t).wait_recv()

        for k in range(4):
            cols = pl.ds(k * 128, 128)
            average = wide(a2a, t, pl.ds(4 * k, 4)).reshape(64, 128) / F32(8)
            moved = outer_momentum * mom[t, :, cols] + average
            params = mas[t, :, cols] - outer_rate * (average + outer_momentum * moved)
            omom[t, :, cols] = moved
            omas[t, :, cols] = params
            ret[t, pl.ds(4 * k, 4)] = params.astype(BF16).reshape(4, 16, 128)

        @pl.when(t > 0)
        def _():
            back(t).start()
            go(t).wait_send()

        @pl.when(t == 0)
        def _():
            back_own().start()

        for copy in store_m(t):
            copy.start()

    def sixth(t):
        @pl.when(t > 0)
        def _():
            back(t, True).wait_recv()

        @pl.when(t == 0)
        def _():
            back_own().wait()

        for i in range(3):
            ag(t, i).start()

        @pl.when(t > 0)
        def _():
            back(t).wait_send()

    def seventh(t):
        for i in range(3):
            ag(t, i, True).wait_recv()
        for i in range(3, 7):
            ag(t, i).start()
        for i in range(3):
            ag(t, i).wait_send()

    def eighth(t):
        for i in range(3, 7):
            ag(t, i, True).wait_recv()
        for i in range(7, 10):
            ag(t, i).start()
        for i in range(3, 7):
            ag(t, i).wait_send()

    def ninth(t):
        for i in range(7, 10):
            ag(t, i, True).wait_recv()
        for i in range(7, 10):
            ag(t, i).wait_send()
        for copy in store_m(t):
            copy.wait()

    for p in range(UNITS // 2):
        load_g(p).start()

    barrier = pltpu.get_barrier_semaphore()
    friends = [right, left, side] + [partner(t) for t in range(1, UNITS)]
    for device in friends:
        pl.semaphore_signal(barrier, inc=1, device_id=device, device_id_type=MESH)

    def start_m(t, _):
        for copy in load_m(t):
            copy.start()
        return 0

    lax.fori_loop(0, UNITS, start_m, 0)
    decode(0)
    pl.semaphore_wait(barrier, len(friends))

    stages = (first, second, third, fourth, fifth, sixth, seventh, eighth, ninth)

    def step(s, _):
        for lag, stage in enumerate(stages):

            @pl.when((s >= lag) & (s < UNITS + lag))
            def _(lag=lag, stage=stage):
                stage(s - lag)

            if lag == 0:

                @pl.when((s % 2 == 1) & (s < UNITS - 1))
                def _():
                    decode((s + 1) // 2)

        return 0

    lax.fori_loop(0, UNITS + len(stages) - 1, step, 0)


def order_kernel(layout, raw, out):
    for j in range(UNITS):
        for k in range(4):
            out[pl.ds(j * 64, 64), pl.ds(k * 128, 128)] = raw[j, 0, 0, pl.ds(4 * k, 4)].reshape(64, 128)


def per_device(pseudo_grads, exponents, master, momentum, layout):
    tiles = (TILES, 16, 128)
    vmem = lambda *shape: pltpu.VMEM(shape + (16, 128), BF16)
    dma = lambda *shape: pltpu.SemaphoreType.DMA(shape)
    far = pl.BlockSpec(memory_space=pl.ANY)
    raw, new_master, new_momentum = pl.pallas_call(
        step_kernel,
        out_shape=(
            jax.ShapeDtypeStruct((UNITS, 2, 4) + tiles, BF16),
            jax.ShapeDtypeStruct(master.shape, F32),
            jax.ShapeDtypeStruct(master.shape, F32),
        ),
        in_specs=[far, pl.BlockSpec(memory_space=pltpu.VMEM), far, far],
        out_specs=(far, far, far),
        scratch_shapes=[
            pltpu.VMEM((UNITS // 2, 8, 128, 512), BF16),
            vmem(UNITS, 2, 4, TILES),
            vmem(UNITS, 2, XP),
            vmem(UNITS, 2, XT - XP),
            vmem(UNITS, 4, YT),
            vmem(UNITS, 2, XT),
            vmem(UNITS, 2, XT),
            vmem(UNITS, YP),
            vmem(UNITS, YT - YP),
            vmem(UNITS, XT),
            vmem(UNITS, YT),
            vmem(UNITS, YT),
            vmem(UNITS, TILES),
            vmem(UNITS, TILES),
        ]
        + [pltpu.VMEM((UNITS, 64, 512), F32)] * 4
        + [
            dma(UNITS // 2),
            dma(2, UNITS),
            dma(2, UNITS),
            pltpu.SemaphoreType.DMA,
            dma(UNITS, 10),
            dma(UNITS, 10),
            dma(UNITS),
            dma(UNITS),
            dma(UNITS),
            dma(UNITS),
            dma(UNITS, 10),
            dma(UNITS, 10),
        ],
        compiler_params=pltpu.CompilerParams(
            collective_id=0, has_side_effects=True, vmem_limit_bytes=56 * 2**20
        ),
        name="sum_update_gather",
    )(pseudo_grads.reshape(8, 8, 128, 512), exponents[0].T, master, momentum)

    island = pl.pallas_call(
        order_kernel,
        out_shape=jax.ShapeDtypeStruct((8192, 512), BF16),
        grid_spec=pltpu.PrefetchScalarGridSpec(
            num_scalar_prefetch=1,
            grid=(8,),
            in_specs=[
                pl.BlockSpec(
                    (UNITS, 1, 1) + tiles, lambda s, layout: (0, layout[s] // 4, layout[s] % 4, 0, 0, 0)
                )
            ],
            out_specs=pl.BlockSpec((1024, 512), lambda s, layout: (s, 0)),
        ),
        compiler_params=pltpu.CompilerParams(vmem_limit_bytes=32 * 2**20),
        name="layer_order",
    )(layout, raw)
    return new_master, new_momentum, island


def solution(mesh):
    rows = P(("replica", "fsdp"), None)
    grads = P("replica", None, "fsdp")
    return jax.shard_map(
        per_device,
        mesh=mesh,
        in_specs=(grads, grads, rows, rows, P()),
        out_specs=(rows, rows, P(None, "fsdp")),
        check_vma=False,
    )
```

time: 305 us -> 148 us (0.49)
  waiting for transfers between devices: 182 us -> 0 us
  Pallas kernels: 0 us -> 140 us
  blocking collectives: 57 us -> 0 us
  other arithmetic: 22.1 us -> 0 us
  local copies, waits for them, and re-layouts: 29 us -> 7.05 us
  between operations: 14.1 us -> 0.67 us
    pallas_call x0 -> x2, Pallas kernels: none -> 140 us  [the longest x1 134 us: per_device(): pl.pallas_call(step_kernel, out_shape=(jax.ShapeDtypeStruct((UNITS, 2, 4)...]
    reduce_scatter x1 -> x0, waiting for transfers between devices: 95.2 us -> none  [per_device(): lax.psum_scatter(decode(coded, coded_exp).astype(jnp.bfloat16), 'replica'...]
    all_gather x1 -> x0, waiting for transfers between devices: 86.4 us -> none  [per_device(): island = lax.all_gather(local_rows, 'replica', axis=0, tiled=True)]
    all_to_all x2 -> x0, blocking collectives: 57 us -> none  [the longest x1 35.7 us: per_device(): lax.all_to_all(partial_sum, 'fsdp', split_axis=0, concat_axis=1, tiled=True)]
    mul x1 -> x0, local copies, waits for them, and re-layouts: 15.9 us -> none  [decode(): return (blocks * block_scale(exponents)[..., None]).reshape(shape)]
    convert_element_type x2 -> x0, other arithmetic: 11.8 us -> none  [the longest x1 9.28 us: per_device(): decode(coded, coded_exp).astype(jnp.bfloat16)]
    select_n x3 -> x0, other arithmetic: 8.51 us -> none  [the longest x2 7.47 us: per_device(): island_params = jnp.take(grouped, layout, axis=0).reshape(island.shape)]
    gather x1 -> x0, local copies, waits for them, and re-layouts: 8.06 us -> none  [per_device(): island_params = jnp.take(grouped, layout, axis=0).reshape(island.shape)]
  transfers between devices with their start and end apart: 2 -> 0, of which waited for: 2 -> 0; matrix products, arithmetic and copies ran while one was open for 0% -> 0% of each run, Pallas kernels for 0% -> 0%
where the time goes in v1:
time: 148 us; the launch traced here: 147 us
  Pallas kernels  140 us (95%)
  local copies, waits for them, and re-layouts  7.05 us (5%)
    pallas_call x1, Pallas kernels, per_device(): pl.pallas_call(step_kernel, out_shape=(jax.ShapeDtypeStruct((UNITS, 2, 4)...  134 us
    unnamed x10, local copies, waits for them, and re-layouts  7.05 us
    pallas_call x1, Pallas kernels, per_device(): pl.pallas_call(order_kernel, out_shape=jax.ShapeDtypeStruct((8192, 512),...  5.84 us

profile of v1, /device:TPU:0, one launch (start us, length us, event | category | flops | bytes accessed | tf_op | source)
XLA Modules:
  0.0 147.3 jit_solution(4069810420894232503)
XLA Ops:
  0.6 0.0 copy-start.1
  0.6 133.8 %sum_update_gather.1 = (bf16[16,2,4,16,16,128]{5,4,3,2,1,0:T(8,128)(2,1)}, f32[64,8192]{1,0:T(8,128)}, f32[64,8192]{1,0:T(8,128)}) custom-call(bf16[8,8,128,512]{3,2,1,0:T(8,128)(2,1)} %bitcast.4, s32[4,8192]{1,0:T(4,128)} %bitcast.5, f32[64,8192]{1,0:T(8,128)} %master.1, f32[64,8192]{1,0:T(8,128)} %momentum.1), custom_call_target="tpu_custom_call" | custom-call | tf_op jit(solution)/shard_map/sum_update_gather/pallas_call | solution.py:329
  134.4 0.0 copy-done.1
  134.4 0.0 copy-start
  134.4 3.4 %copy-done = bf16[16,2,4,16,16,128]{5,4,3,2,1,0:T(8,128)(2,1)S(1)} copy-done((bf16[16,2,4,16,16,128]{5,4,3,2,1,0:T(8,128)(2,1)S(1)}, bf16[16,2,4,16,16,128]{5,4,3,2,1,0:T(8,128)(2,1)}, u32[]{:S(2)}) %copy-start) | copy-done | bytes 8388632
  137.8 0.0 copy-start.3
  137.8 5.8 %layer_order.1 = bf16[8192,512]{1,0:T(8,128)(2,1)} custom-call(s32[8]{0:T(128)S(1)} %copy-done.1, bf16[16,2,4,16,16,128]{5,4,3,2,1,0:T(8,128)(2,1)S(1)} %copy-done), custom_call_target="tpu_custom_call" | custom-call | tf_op jit(solution)/shard_map/layer_order/pallas_call | solution.py:375
  143.7 0.0 copy-done.3
  143.7 0.0 copy-start.2
  143.7 1.3 copy.10
  145.0 1.0 copy-done.2
  146.0 1.3 copy.11
Async XLA Ops:
  0.6 133.8 %copy-start.1 = (s32[8]{0:T(128)S(1)}, s32[8]{0:T(128)}, u32[]{:S(2)}) copy-start(s32[8]{0:T(128)} %layout.1) | copy-start | bytes 100
  134.4 3.4 %copy-start = (bf16[16,2,4,16,16,128]{5,4,3,2,1,0:T(8,128)(2,1)S(1)}, bf16[16,2,4,16,16,128]{5,4,3,2,1,0:T(8,128)(2,1)}, u32[]{:S(2)}) copy-start(bf16[16,2,4,16,16,128]{5,4,3,2,1,0:T(8,128)(2,1)} %get-tuple-element.8.raw) | copy-start | bytes 25165828
  137.8 5.8 %copy-start.3 = (f32[64,8192]{1,0:T(8,128)S(1)}, f32[64,8192]{1,0:T(8,128)}, u32[]{:S(2)}) copy-start(f32[64,8192]{1,0:T(8,128)} %get-tuple-element.12) | copy-start | bytes 6291460
  143.7 2.3 %copy-start.2 = (f32[64,8192]{1,0:T(8,128)S(1)}, f32[64,8192]{1,0:T(8,128)}, u32[]{:S(2)}) copy-start(f32[64,8192]{1,0:T(8,128)} %get-tuple-element.13) | copy-start | bytes 6291460

commit v2 on v1

--- a/solution.py
+++ b/solution.py
@@ -18,6 +18,7 @@
 YT = TILES - XT
 YP = 3
 YM = XT + YP
+LAGS = (0, 3, 6, 9, 12, 15, 18, 21, 24)
 
 
 def bit(v, b):
@@ -47,7 +48,8 @@
 ):
     rep, fs = lax.axis_index("replica"), lax.axis_index("fsdp")
     x, yl = rep % 4, rep // 4
-    xp, xm, xo = (x + 1) % 4, (x + 3) % 4, (x + 2) % 4
+    turn = 2 * (fs % 2)
+    xp, xm, xo = (x + 1 + turn) % 4, (x + 3 + turn) % 4, (x + 2) % 4
     right, left, side = (yl * 4 + xp, fs), (yl * 4 + xm, fs), ((1 - yl) * 4 + x, fs)
 
     def own(t):
@@ -70,8 +72,8 @@
 
     def store_m(t):
         return (
-            pltpu.make_async_copy(omas.at[t], new_master.at[:, columns(t)], o_sem.at[0, t]),
-            pltpu.make_async_copy(omom.at[t], new_momentum.at[:, columns(t)], o_sem.at[1, t]),
+            pltpu.make_async_copy(omas.at[t], new_master.at[xor16(fs, t)], o_sem.at[0, t]),
+            pltpu.make_async_copy(omom.at[t], new_momentum.at[xor16(fs, t)], o_sem.at[1, t]),
         )
 
     def remote(src, dst, send, recv, device):
@@ -141,10 +143,10 @@
             rows = pl.ds(pl.multiple_of(l * 1024 + base, 128), 128)
             scale = block_scale(expt[:, rows])
             scale = jnp.concatenate([scale, jnp.zeros((4, 128), F32)], axis=0)
-            spread = lax.dot_general(scale, pick, (((0,), (0,)), ((), ())), preferred_element_type=F32)
+            spread = lax.dot_general(scale, pick, (((0,), (0,)), ((), ())), preferred_element_type=F32).astype(BF16)
             for k in range(4):
                 cols = pl.ds(k * 128, 128)
-                piece = (graw[p, l, :, cols].astype(F32) * spread[:, k * 128 : (k + 1) * 128]).astype(BF16)
+                piece = graw[p, l, :, cols] * spread[:, k * 128 : (k + 1) * 128]
                 piece = piece.reshape(2, 4, 16, 128)
                 for h in range(2):
                     dec[2 * p + flip(odd, h), l // 4, l % 4, pl.ds(4 * k, 4)] = piece[h]
@@ -298,7 +300,7 @@
     stages = (first, second, third, fourth, fifth, sixth, seventh, eighth, ninth)
 
     def step(s, _):
-        for lag, stage in enumerate(stages):
+        for lag, stage in zip(LAGS, stages):
 
             @pl.when((s >= lag) & (s < UNITS + lag))
             def _(lag=lag, stage=stage):
@@ -312,13 +314,29 @@
 
         return 0
 
-    lax.fori_loop(0, UNITS + len(stages) - 1, step, 0)
-
-
-def order_kernel(layout, raw, out):
-    for j in range(UNITS):
-        for k in range(4):
-            out[pl.ds(j * 64, 64), pl.ds(k * 128, 128)] = raw[j, 0, 0, pl.ds(4 * k, 4)].reshape(64, 128)
+    lax.fori_loop(0, UNITS + LAGS[-1], step, 0)
+
+
+def order_kernel(layout, raw, mas, mom, out, new_master, new_momentum, staged, sems, more_sems):
+    copies = []
+    for f in range(UNITS):
+        for i, (ref, to) in enumerate(((mas, new_master), (mom, new_momentum))):
+            copies.append(pltpu.make_async_copy(ref.at[f], to.at[:, pl.ds(f * 512, 512)], more_sems.at[i, f]))
+            copies[-1].start()
+    for s in range(8):
+        l = layout[s]
+
+        def one(j, _, s=s, l=l):
+            rows = pl.ds(pl.multiple_of(j * 64, 64), 64)
+            for k in range(4):
+                staged[s, rows, pl.ds(128 * k, 128)] = raw[j, l // 4, l % 4, pl.ds(4 * k, 4)].reshape(64, 128)
+            return 0
+
+        lax.fori_loop(0, UNITS, one, 0)
+        copies.append(pltpu.make_async_copy(staged.at[s], out.at[pl.ds(s * 1024, 1024)], sems.at[s]))
+        copies[-1].start()
+    for copy in copies:
+        copy.wait()
 
 
 def per_device(pseudo_grads, exponents, master, momentum, layout):
@@ -326,12 +344,12 @@
     vmem = lambda *shape: pltpu.VMEM(shape + (16, 128), BF16)
     dma = lambda *shape: pltpu.SemaphoreType.DMA(shape)
     far = pl.BlockSpec(memory_space=pl.ANY)
-    raw, new_master, new_momentum = pl.pallas_call(
+    results = pl.pallas_call(
         step_kernel,
         out_shape=(
-            jax.ShapeDtypeStruct((UNITS, 2, 4) + tiles, BF16),
-            jax.ShapeDtypeStruct(master.shape, F32),
-            jax.ShapeDtypeStruct(master.shape, F32),
+            pltpu.VMEM((UNITS, 2, 4) + tiles, BF16),
+            pltpu.VMEM((UNITS, 64, 512), F32),
+            pltpu.VMEM((UNITS, 64, 512), F32),
         ),
         in_specs=[far, pl.BlockSpec(memory_space=pltpu.VMEM), far, far],
         out_specs=(far, far, far),
@@ -367,27 +385,25 @@
             dma(UNITS, 10),
         ],
         compiler_params=pltpu.CompilerParams(
-            collective_id=0, has_side_effects=True, vmem_limit_bytes=56 * 2**20
+            collective_id=0, has_side_effects=True, vmem_limit_bytes=48 * 2**20
         ),
         name="sum_update_gather",
     )(pseudo_grads.reshape(8, 8, 128, 512), exponents[0].T, master, momentum)
 
-    island = pl.pallas_call(
+    near = pl.BlockSpec(memory_space=pltpu.VMEM)
+    island, new_master, new_momentum = pl.pallas_call(
         order_kernel,
-        out_shape=jax.ShapeDtypeStruct((8192, 512), BF16),
-        grid_spec=pltpu.PrefetchScalarGridSpec(
-            num_scalar_prefetch=1,
-            grid=(8,),
-            in_specs=[
-                pl.BlockSpec(
-                    (UNITS, 1, 1) + tiles, lambda s, layout: (0, layout[s] // 4, layout[s] % 4, 0, 0, 0)
-                )
-            ],
-            out_specs=pl.BlockSpec((1024, 512), lambda s, layout: (s, 0)),
+        out_shape=(
+            jax.ShapeDtypeStruct((8192, 512), BF16),
+            jax.ShapeDtypeStruct(master.shape, F32),
+            jax.ShapeDtypeStruct(master.shape, F32),
         ),
-        compiler_params=pltpu.CompilerParams(vmem_limit_bytes=32 * 2**20),
+        in_specs=[pl.BlockSpec(memory_space=pltpu.SMEM), near, near, near],
+        out_specs=(far, far, far),
+        scratch_shapes=[pltpu.VMEM((8, 1024, 512), BF16), dma(8), dma(2, UNITS)],
+        compiler_params=pltpu.CompilerParams(vmem_limit_bytes=12 * 2**20),
         name="layer_order",
-    )(layout, raw)
+    )(layout, *results)
     return new_master, new_momentum, island
 
 

time: 148 us -> 133 us (0.90)
  Pallas kernels: 140 us -> 132 us
  local copies, waits for them, and re-layouts: 7.05 us -> 0.01 us
    pallas_call x2, Pallas kernels: 140 us -> 132 us  [the longest x1 126 us: per_device(): pl.pallas_call(step_kernel, out_shape=(pltpu.VMEM((UNITS, 2, 4) + tiles,...]
    unnamed x10 -> x2, local copies, waits for them, and re-layouts: 7.05 us -> 0.01 us
where the time goes in v2:
time: 133 us
  Pallas kernels  132 us (99%)
    pallas_call x1, Pallas kernels, per_device(): pl.pallas_call(step_kernel, out_shape=(pltpu.VMEM((UNITS, 2, 4) + tiles,...  126 us
    pallas_call x1, Pallas kernels, per_device(): pl.pallas_call(order_kernel, out_shape=(jax.ShapeDtypeStruct((8192, 512),...  5.44 us

profile of v2, /device:TPU:0, one launch (start us, length us, event | category | flops | bytes accessed | tf_op | source)
XLA Modules:
  0.0 132.5 jit_solution(1326375887088702953)
XLA Ops:
  0.6 0.0 copy-start
  0.6 126.4 %sum_update_gather.1 = (bf16[16,2,4,16,16,128]{5,4,3,2,1,0:T(8,128)(2,1)S(1)}, f32[16,64,512]{2,1,0:T(8,128)S(1)}, f32[16,64,512]{2,1,0:T(8,128)S(1)}) custom-call(bf16[8,8,128,512]{3,2,1,0:T(8,128)(2,1)} %bitcast.4, s32[4,8192]{1,0:T(4,128)} %bitcast.5, f32[64,8192]{1,0:T(8,128)} %master.1, f32[64,8192]{1,0:T(8,128)} %momentum.1), custom_call_target="tpu_custom_call" | custom-call | tf_op jit(solution)/shard_map/sum_update_gather/pallas_call | solution.py:347
  127.1 0.0 copy-done
  127.1 5.4 %layer_order.1 = (bf16[8192,512]{1,0:T(8,128)(2,1)}, f32[64,8192]{1,0:T(8,128)}, f32[64,8192]{1,0:T(8,128)}) custom-call(s32[8]{0:T(128)S(1)} %copy-done, bf16[16,2,4,16,16,128]{5,4,3,2,1,0:T(8,128)(2,1)S(1)} %get-tuple-element.9.raw, f32[16,64,512]{2,1,0:T(8,128)S(1)} %get-tuple-element.10.mas, f32[16,64,512]{2,1,0:T(8,128)S(1)} %get-tuple-element.11.mom), custom_call_target="tpu_custom_call" | custom-call | tf_op jit(solution)/shard_map/layer_order/pallas_call | solution.py:394
Async XLA Ops:
  0.6 126.4 %copy-start = (s32[8]{0:T(128)S(1)}, s32[8]{0:T(128)}, u32[]{:S(2)}) copy-start(s32[8]{0:T(128)} %layout.1) | copy-start | bytes 100

commit v3 on v0

v3 whole, which is shorter than its diff:
```python
import jax
import jax.numpy as jnp
from jax import lax
from jax.experimental import pallas as pl
from jax.experimental.pallas import tpu as pltpu
from jax.sharding import PartitionSpec as P

MESH = pl.DeviceIdType.MESH
F32, BF16 = jnp.float32, jnp.bfloat16

outer_rate = 0.7
outer_momentum = 0.9

UNITS = 16
TILES = 16
XT = 9
XP = 5
YT = TILES - XT
YP = 3
YM = XT + YP


ORDER = (
    ("x1", 0), ("y1", 0), ("decode", 0), ("x2", 3), ("y2", 3), ("x3", 6), ("y3", 6), ("z4", 9), ("z5", 12),
    ("gx1", 15), ("gy1", 15), ("gx2", 18), ("gy2", 18), ("gx3", 21), ("gy3", 21),
)


def bit(v, b):
    return lax.rem(lax.div(v, 1 << b), 2)


def flip(a, b):
    return a + b - 2 * a * b


def block_scale(exponents):
    scale = jnp.zeros(exponents.shape, F32)
    for level in range(-6, 2):
        scale = jnp.where(exponents == level, F32(2.0**level), scale)
    return scale


def step_kernel(
    g, expt, master, momentum,
    isl, new_master, new_momentum,
    graw, dec, r1x, r1y, r2x, r2y, r3, a2a, ret, mas, mom,
    g_sem, m_sem, own_sem, send_sem, x1_sem, y1_sem, x2_sem, y2_sem, r3_sem, a_sem, b_sem,
    gx1_sem, gy1_sem, gx2_sem, gy2_sem, gx3_sem, gy3_sem,
):
    rep, fs = lax.axis_index("replica"), lax.axis_index("fsdp")
    x, yl = lax.rem(rep, 4), lax.div(rep, 4)
    turn = 2 * lax.rem(fs, 2)
    xp, xm, xo = lax.rem(x + 1 + turn, 4), lax.rem(x + 3 + turn, 4), lax.rem(x + 2, 4)
    right, left, side = (yl * 4 + xp, fs), (yl * 4 + xm, fs), ((1 - yl) * 4 + x, fs)
    swaps = [(1 - 2 * bit(fs, b)) * (1 << b) for b in range(4)]
    every = slice(None)
    tx, ty = pl.ds(0, XT), pl.ds(XT, YT)
    txp, txm = pl.ds(0, XP), pl.ds(XP, XT - XP)
    typ, tym = pl.ds(XT, YP), pl.ds(YM, YT - YP)

    def other(t):
        return fs + sum(bit(t, b) * swaps[b] for b in range(4))

    def own(t):
        return flip(yl, bit(t, 1))

    def partner(t):
        return (own(t) * 4 + x, other(t))

    def columns(t):
        return pl.ds(pl.multiple_of(other(t) * 512, 512), 512)

    def load_g(p):
        return pltpu.make_async_copy(g.at[:, lax.div(other(2 * p), 2)], graw.at[p], g_sem.at[p])

    loads = (
        pltpu.make_async_copy(master, mas, m_sem.at[0]),
        pltpu.make_async_copy(momentum, mom, m_sem.at[1]),
    )

    def remote(src, dst, send, recv, device):
        return pltpu.make_async_remote_copy(
            src_ref=src, dst_ref=dst, send_sem=send_sem.at[send], recv_sem=recv, device_id=device, device_id_type=MESH
        )

    def send(src, dst, recv, device):
        remote(src, dst, 0, recv, device).start()

    def spread(ref, recv, device):
        remote(ref, ref, 1, recv, device).start()

    def arrived(ref, recv):
        remote(ref, ref, 0, recv, right).wait_recv()

    def wide(ref, *at):
        return ref[at].astype(F32)

    def z4_copy(t):
        return remote(dec.at[t, own(t), x], a2a.at[t], 2, a_sem.at[t], partner(t))

    def z5_copy(t):
        return remote(ret.at[t], isl.at[fs, yl, x], 3, b_sem.at[t], partner(t))

    def z5_own():
        return pltpu.make_async_copy(ret.at[0], isl.at[fs, yl, x], own_sem)

    lane_block = lax.broadcasted_iota(jnp.int32, (8, 512), 1) // 128
    pick = (lane_block == lax.broadcasted_iota(jnp.int32, (8, 512), 0)).astype(F32)

    def decode(p):
        load_g(p).wait()
        base = lax.div(other(2 * p), 2) * 128
        odd = lax.rem(fs, 2)

        def one(l, _):
            rows = pl.ds(pl.multiple_of(l * 1024 + base, 128), 128)
            scale = block_scale(expt[:, rows])
            scale = jnp.concatenate([scale, jnp.zeros((4, 128), F32)], axis=0)
            scales = lax.dot_general(scale, pick, (((0,), (0,)), ((), ())), preferred_element_type=F32).astype(BF16)
            for k in range(4):
                piece = graw[p, l, :, pl.ds(k * 128, 128)] * scales[:, k * 128 : (k + 1) * 128]
                piece = piece.reshape(2, 4, 16, 128)
                for h in range(2):
                    dec[2 * p + flip(odd, h), lax.div(l, 4), lax.rem(l, 4), pl.ds(4 * k, 4)] = piece[h]
            return 0

        lax.fori_loop(0, 8, one, 0)

    def x1(t):
        send(dec.at[t, every, xo, txp], r1x.at[t, every, txp], x1_sem.at[t], right)
        send(dec.at[t, every, xo, txm], r1x.at[t, every, txm], x1_sem.at[t], left)

    def y1(t):
        send(dec.at[t, 1 - own(t), every, ty], r1y.at[t], y1_sem.at[t], side)

    def x2(t):
        arrived(r1x.at[t], x1_sem.at[t])
        at = (t, every, xp, txp)
        dec[at] = (wide(dec, *at) + wide(r1x, t, every, txp)).astype(BF16)
        send(dec.at[t, every, xp, tx], r2x.at[t, 0], x2_sem.at[t], right)
        at = (t, every, xm, txm)
        dec[at] = (wide(dec, *at) + wide(r1x, t, every, txm)).astype(BF16)
        send(dec.at[t, every, xm, tx], r2x.at[t, 1], x2_sem.at[t], left)

    def y2(t):
        arrived(r1y.at[t], y1_sem.at[t])
        o = own(t)
        at = (t, o, every, ty)
        dec[at] = (wide(dec, *at) + wide(r1y, t)).astype(BF16)
        send(dec.at[t, o, xo, typ], r2y.at[t, pl.ds(0, YP)], y2_sem.at[t], right)
        send(dec.at[t, o, xo, tym], r2y.at[t, pl.ds(YP, YT - YP)], y2_sem.at[t], left)

    def x3(t):
        arrived(r2x.at[t], x2_sem.at[t])
        o = 1 - own(t)
        at = (t, o, x, tx)
        dec[at] = (wide(dec, *at) + wide(r2x, t, 0, o) + wide(r2x, t, 1, o)).astype(BF16)
        send(dec.at[at], r3.at[t, tx], r3_sem.at[t], side)

    def y3(t):
        arrived(r2y.at[t], y2_sem.at[t])
        o = own(t)
        at = (t, o, xp, typ)
        dec[at] = (wide(dec, *at) + wide(r2y, t, pl.ds(0, YP))).astype(BF16)
        send(dec.at[t, o, xp, ty], r3.at[t, pl.ds(XT, YT)], r3_sem.at[t], right)
        at = (t, o, xm, tym)
        dec[at] = (wide(dec, *at) + wide(r2y, t, pl.ds(YP, YT - YP))).astype(BF16)
        send(dec.at[t, o, xm, ty], r3.at[t, pl.ds(XT + YT, YT)], r3_sem.at[t], left)

    def z4(t):
        arrived(r3.at[t], r3_sem.at[t])
        o = own(t)
        at = (t, o, x, tx)
        dec[at] = (wide(dec, *at) + wide(r2x, t, 0, o) + wide(r2x, t, 1, o) + wide(r3, t, tx)).astype(BF16)
        at = (t, o, x, ty)
        dec[at] = (wide(dec, *at) + wide(r3, t, ty) + wide(r3, t, pl.ds(XT + YT, YT))).astype(BF16)

        @pl.when(t > 0)
        def _():
            z4_copy(t).start()

        @pl.when(t == 0)
        def _():
            a2a[0] = dec[0, yl, x]

    def z5(t):
        @pl.when(t > 0)
        def _():
            z4_copy(t).wait_recv()

        @pl.when(t == 0)
        def _():
            for load in loads:
                load.wait()

        for k in range(4):
            cols = pl.ds(pl.multiple_of(other(t) * 512 + k * 128, 128), 128)
            average = wide(a2a, t, pl.ds(4 * k, 4)).reshape(64, 128) / F32(8)
            moved = outer_momentum * mom[:, cols] + average
            params = mas[:, cols] - outer_rate * (average + outer_momentum * moved)
            new_momentum[:, cols] = moved
            new_master[:, cols] = params
            ret[t, pl.ds(4 * k, 4)] = params.astype(BF16).reshape(4, 16, 128)

        @pl.when(t > 0)
        def _():
            z5_copy(t).start()

        @pl.when(t == 0)
        def _():
            z5_own().start()

    def ready(t):
        @pl.when(t > 0)
        def _():
            arrived(isl.at[other(t), own(t), x], b_sem.at[t])

        @pl.when(t == 0)
        def _():
            z5_own().wait()

    def gx1(t):
        ready(t)
        spread(isl.at[other(t), own(t), x, tx], gx1_sem.at[t], side)

    def gy1(t):
        at = isl.at[other(t), own(t), x, ty]
        spread(at, gy1_sem.at[t], right)
        spread(at, gy1_sem.at[t], left)

    def gx2(t):
        j = other(t)
        arrived(isl.at[j, 1 - own(t), x, tx], gx1_sem.at[t])
        at = isl.at[j, every, x, tx]
        spread(at, gx2_sem.at[t], right)
        spread(at, gx2_sem.at[t], left)

    def gy2(t):
        j, o = other(t), own(t)
        arrived(isl.at[j, every, x, ty], gy1_sem.at[t])
        spread(isl.at[j, o, xm, typ], gy2_sem.at[t], right)
        spread(isl.at[j, o, xp, tym], gy2_sem.at[t], left)

    def gx3(t):
        j = other(t)
        arrived(isl.at[j, every, pl.ds(0, 2), tx], gx2_sem.at[t])
        spread(isl.at[j, every, xm, txp], gx3_sem, right)
        spread(isl.at[j, every, xp, txm], gx3_sem, left)

    def gy3(t):
        j, o = other(t), own(t)
        arrived(isl.at[j, o, xo, ty], gy2_sem.at[t])
        spread(isl.at[j, o, every, ty], gy3_sem, side)

    barrier = pltpu.get_barrier_semaphore()
    load_g(0).start()
    friends = [right, left, side] + [partner(jnp.int32(t)) for t in range(1, UNITS)]
    for device in friends:
        pl.semaphore_signal(barrier, inc=1, device_id=device, device_id_type=MESH)
    load_g(1).start()
    decode(0)
    for p in range(2, UNITS // 2):
        load_g(p).start()
    for load in loads:
        load.start()
    pl.semaphore_wait(barrier, len(friends))

    stages = dict(
        x1=x1, y1=y1, x2=x2, y2=y2, x3=x3, y3=y3, z4=z4, z5=z5, gx1=gx1, gy1=gy1, gx2=gx2, gy2=gy2, gx3=gx3, gy3=gy3
    )

    def step(s, _):
        for name, lag in ORDER:
            if name == "decode":

                @pl.when((lax.rem(s, 2) == 1) & (s < UNITS - 1))
                def _():
                    decode(lax.div(s + 1, 2))

            else:

                @pl.when((s >= lag) & (s < UNITS + lag))
                def _(lag=lag, stage=stages[name]):
                    stage(s - lag)

        return 0

    lax.fori_loop(0, UNITS + max(lag for _, lag in ORDER), step, 0)

    arrived(isl.at[every, every, xo, tx], gx3_sem)
    arrived(isl.at[every, 0, every, ty], gy3_sem)
    for i, ref in enumerate(
        (dec.at[every, every, every, pl.ds(0, 14)], isl.at[every, every, every, pl.ds(0, 14)], a2a.at[pl.ds(1, 15)], ret.at[pl.ds(1, 15)])
    ):
        remote(ref, ref, i, gx3_sem, right).wait_send()


def order_kernel(layout, raw, mas, mom, out, new_master, new_momentum, staged, sems):
    copies = [pltpu.make_async_copy(mas, new_master, sems.at[8]), pltpu.make_async_copy(mom, new_momentum, sems.at[9])]
    for copy in copies:
        copy.start()
    for s in range(8):
        l = layout[s]

        def one(j, _, s=s, l=l):
            rows = pl.ds(pl.multiple_of(j * 64, 64), 64)
            for k in range(4):
                staged[s, rows, pl.ds(128 * k, 128)] = raw[j, l // 4, l % 4, pl.ds(4 * k, 4)].reshape(64, 128)
            return 0

        lax.fori_loop(0, UNITS, one, 0)
        copies.append(pltpu.make_async_copy(staged.at[s], out.at[pl.ds(s * 1024, 1024)], sems.at[s]))
        copies[-1].start()
    for copy in copies:
        copy.wait()


def per_device(pseudo_grads, exponents, master, momentum, layout):
    tiles = (TILES, 16, 128)
    vmem = lambda *shape: pltpu.VMEM(shape + (16, 128), BF16)
    dma = lambda *shape: pltpu.SemaphoreType.DMA(shape)
    far = pl.BlockSpec(memory_space=pl.ANY)
    near = pl.BlockSpec(memory_space=pltpu.VMEM)
    results = pl.pallas_call(
        step_kernel,
        out_shape=(
            pltpu.VMEM((UNITS, 2, 4) + tiles, BF16),
            pltpu.VMEM(master.shape, F32),
            pltpu.VMEM(master.shape, F32),
        ),
        in_specs=[far, near, far, far],
        out_specs=(far, near, near),
        scratch_shapes=[
            pltpu.VMEM((UNITS // 2, 8, 128, 512), BF16),
            vmem(UNITS, 2, 4, TILES),
            vmem(UNITS, 2, XT),
            vmem(UNITS, 4, YT),
            vmem(UNITS, 2, 2, XT),
            vmem(UNITS, YT),
            vmem(UNITS, XT + 2 * YT),
            vmem(UNITS, TILES),
            vmem(UNITS, TILES),
            pltpu.VMEM(master.shape, F32),
            pltpu.VMEM(master.shape, F32),
            dma(UNITS // 2),
            dma(2),
            pltpu.SemaphoreType.DMA,
            dma(4),
        ]
        + [dma(UNITS)] * 11
        + [pltpu.SemaphoreType.DMA] * 2,
        compiler_params=pltpu.CompilerParams(
            collective_id=0, has_side_effects=True, vmem_limit_bytes=48 * 2**20
        ),
        name="sum_update_gather",
    )(pseudo_grads.reshape(8, 8, 128, 512), exponents[0].T, master, momentum)

    island, new_master, new_momentum = pl.pallas_call(
        order_kernel,
        out_shape=(
            jax.ShapeDtypeStruct((8192, 512), BF16),
            jax.ShapeDtypeStruct(master.shape, F32),
            jax.ShapeDtypeStruct(master.shape, F32),
        ),
        in_specs=[pl.BlockSpec(memory_space=pltpu.SMEM), near, near, near],
        out_specs=(far, far, far),
        scratch_shapes=[pltpu.VMEM((8, 1024, 512), BF16), dma(10)],
        compiler_params=pltpu.CompilerParams(vmem_limit_bytes=12 * 2**20),
        name="layer_order",
    )(layout, *results)
    return new_master, new_momentum, island


def solution(mesh):
    rows = P(("replica", "fsdp"), None)
    grads = P("replica", None, "fsdp")
    return jax.shard_map(
        per_device,
        mesh=mesh,
        in_specs=(grads, grads, rows, rows, P()),
        out_specs=(rows, rows, P(None, "fsdp")),
        check_vma=False,
    )
```

time: 305 us -> 127 us (0.42)
  waiting for transfers between devices: 182 us -> 0 us
  Pallas kernels: 0 us -> 126 us
  blocking collectives: 57 us -> 0 us
  local copies, waits for them, and re-layouts: 29 us -> 0.01 us
  other arithmetic: 22.1 us -> 0 us
  between operations: 14.1 us -> 0.66 us
    pallas_call x0 -> x2, Pallas kernels: none -> 126 us  [the longest x1 121 us: per_device(): pl.pallas_call(step_kernel, out_shape=(pltpu.VMEM((UNITS, 2, 4) + tiles,...]
    reduce_scatter x1 -> x0, waiting for transfers between devices: 95.2 us -> none  [per_device(): lax.psum_scatter(decode(coded, coded_exp).astype(jnp.bfloat16), 'replica'...]
    all_gather x1 -> x0, waiting for transfers between devices: 86.4 us -> none  [per_device(): island = lax.all_gather(local_rows, 'replica', axis=0, tiled=True)]
    all_to_all x2 -> x0, blocking collectives: 57 us -> none  [the longest x1 35.7 us: per_device(): lax.all_to_all(partial_sum, 'fsdp', split_axis=0, concat_axis=1, tiled=True)]
    mul x1 -> x0, local copies, waits for them, and re-layouts: 15.9 us -> none  [decode(): return (blocks * block_scale(exponents)[..., None]).reshape(shape)]
    convert_element_type x2 -> x0, other arithmetic: 11.8 us -> none  [the longest x1 9.28 us: per_device(): decode(coded, coded_exp).astype(jnp.bfloat16)]
    select_n x3 -> x0, other arithmetic: 8.51 us -> none  [the longest x2 7.47 us: per_device(): island_params = jnp.take(grouped, layout, axis=0).reshape(island.shape)]
    gather x1 -> x0, local copies, waits for them, and re-layouts: 8.06 us -> none  [per_device(): island_params = jnp.take(grouped, layout, axis=0).reshape(island.shape)]
  transfers between devices with their start and end apart: 2 -> 0, of which waited for: 2 -> 0; matrix products, arithmetic and copies ran while one was open for 0% -> 0% of each run, Pallas kernels for 0% -> 0%
where the time goes in v3:
time: 127 us; the launch traced here: 126 us
  Pallas kernels  126 us (99%)
    pallas_call x1, Pallas kernels, per_device(): pl.pallas_call(step_kernel, out_shape=(pltpu.VMEM((UNITS, 2, 4) + tiles,...  121 us
    pallas_call x1, Pallas kernels, per_device(): pl.pallas_call(order_kernel, out_shape=(jax.ShapeDtypeStruct((8192, 512),...  5.19 us

profile of v3, /device:TPU:0, one launch (start us, length us, event | category | flops | bytes accessed | tf_op | source)
XLA Modules:
  0.0 126.5 jit_solution(163538382923199088)
XLA Ops:
  0.6 0.0 copy-start
  0.6 120.6 %sum_update_gather.1 = (bf16[16,2,4,16,16,128]{5,4,3,2,1,0:T(8,128)(2,1)S(1)}, f32[64,8192]{1,0:T(8,128)S(1)}, f32[64,8192]{1,0:T(8,128)S(1)}) custom-call(bf16[8,8,128,512]{3,2,1,0:T(8,128)(2,1)} %bitcast.4, s32[4,8192]{1,0:T(4,128)} %bitcast.5, f32[64,8192]{1,0:T(8,128)} %master.1, f32[64,8192]{1,0:T(8,128)} %momentum.1), custom_call_target="tpu_custom_call" | custom-call | tf_op jit(solution)/shard_map/sum_update_gather/pallas_call | solution.py:325
  121.3 0.0 copy-done
  121.3 5.2 %layer_order.1 = (bf16[8192,512]{1,0:T(8,128)(2,1)}, f32[64,8192]{1,0:T(8,128)}, f32[64,8192]{1,0:T(8,128)}) custom-call(s32[8]{0:T(128)S(1)} %copy-done, bf16[16,2,4,16,16,128]{5,4,3,2,1,0:T(8,128)(2,1)S(1)} %get-tuple-element.9.raw, f32[64,8192]{1,0:T(8,128)S(1)} %get-tuple-element.10.mas, f32[64,8192]{1,0:T(8,128)S(1)} %get-tuple-element.11.mom), custom_call_target="tpu_custom_call" | custom-call | tf_op jit(solution)/shard_map/layer_order/pallas_call | solution.py:359
Async XLA Ops:
  0.6 120.6 %copy-start = (s32[8]{0:T(128)S(1)}, s32[8]{0:T(128)}, u32[]{:S(2)}) copy-start(s32[8]{0:T(128)} %layout.1) | copy-start | bytes 100

commit v4 on v3

--- a/solution.py
+++ b/solution.py
@@ -21,8 +21,7 @@
 
 
 ORDER = (
-    ("x1", 0), ("y1", 0), ("decode", 0), ("x2", 3), ("y2", 3), ("x3", 6), ("y3", 6), ("z4", 9), ("z5", 12),
-    ("gx1", 15), ("gy1", 15), ("gx2", 18), ("gy2", 18), ("gx3", 21), ("gy3", 21),
+    ("x1", 0), ("y1", 0), ("decode", 0), ("x2", 3), ("y2", 4), ("x3", 6), ("y3", 6), ("z4", 9), ("z5", 11), ("gx1", 13), ("gy1", 13), ("gx2", 16), ("gy2", 15), ("gx3", 22), ("gy3", 17),
 )
 
 
@@ -42,10 +41,10 @@
 
 
 def step_kernel(
-    g, expt, master, momentum,
+    g, exps, master, momentum,
     isl, new_master, new_momentum,
-    graw, dec, r1x, r1y, r2x, r2y, r3, a2a, ret, mas, mom,
-    g_sem, m_sem, own_sem, send_sem, x1_sem, y1_sem, x2_sem, y2_sem, r3_sem, a_sem, b_sem,
+    graw, expt, dec, r1x, r1y, r2x, r2y, r3, a2a, ret, mas, mom,
+    g_sem, e_sem, m_sem, own_sem, send_sem, x1_sem, y1_sem, x2_sem, y2_sem, r3_sem, a_sem, b_sem,
     gx1_sem, gy1_sem, gx2_sem, gy2_sem, gx3_sem, gy3_sem,
 ):
     rep, fs = lax.axis_index("replica"), lax.axis_index("fsdp")
@@ -74,6 +73,11 @@
     def load_g(p):
         return pltpu.make_async_copy(g.at[:, lax.div(other(2 * p), 2)], graw.at[p], g_sem.at[p])
 
+    def load_half(h, sem):
+        at = pl.ds(4 * h, 4)
+        return pltpu.make_async_copy(g.at[at, lax.div(fs, 2)], graw.at[0, at], g_sem.at[sem])
+
+    load_e = pltpu.make_async_copy(exps, expt, e_sem)
     loads = (
         pltpu.make_async_copy(master, mas, m_sem.at[0]),
         pltpu.make_async_copy(momentum, mom, m_sem.at[1]),
@@ -108,24 +112,28 @@
     lane_block = lax.broadcasted_iota(jnp.int32, (8, 512), 1) // 128
     pick = (lane_block == lax.broadcasted_iota(jnp.int32, (8, 512), 0)).astype(F32)
 
-    def decode(p):
-        load_g(p).wait()
+    def decode_half(p, y):
         base = lax.div(other(2 * p), 2) * 128
         odd = lax.rem(fs, 2)
-
-        def one(l, _):
-            rows = pl.ds(pl.multiple_of(l * 1024 + base, 128), 128)
+        for i in range(4):
+            rows = pl.ds(pl.multiple_of((4 * y + i) * 1024 + base, 128), 128)
             scale = block_scale(expt[:, rows])
             scale = jnp.concatenate([scale, jnp.zeros((4, 128), F32)], axis=0)
             scales = lax.dot_general(scale, pick, (((0,), (0,)), ((), ())), preferred_element_type=F32).astype(BF16)
             for k in range(4):
-                piece = graw[p, l, :, pl.ds(k * 128, 128)] * scales[:, k * 128 : (k + 1) * 128]
+                piece = graw[p, 4 * y + i, :, pl.ds(k * 128, 128)] * scales[:, k * 128 : (k + 1) * 128]
                 piece = piece.reshape(2, 4, 16, 128)
                 for h in range(2):
-                    dec[2 * p + flip(odd, h), lax.div(l, 4), lax.rem(l, 4), pl.ds(4 * k, 4)] = piece[h]
+                    dec[2 * p + flip(odd, h), y, i, pl.ds(4 * k, 4)] = piece[h]
+
+    def decode(p):
+        load_g(p).wait()
+
+        def one(y, _):
+            decode_half(p, y)
             return 0
 
-        lax.fori_loop(0, 8, one, 0)
+        lax.fori_loop(0, 2, one, 0)
 
     def x1(t):
         send(dec.at[t, every, xo, txp], r1x.at[t, every, txp], x1_sem.at[t], right)
@@ -254,17 +262,41 @@
         spread(isl.at[j, o, every, ty], gy3_sem, side)
 
     barrier = pltpu.get_barrier_semaphore()
-    load_g(0).start()
+    load_e.start()
+    load_half(1 - yl, 0).start()
+    load_half(yl, UNITS // 2).start()
     friends = [right, left, side] + [partner(jnp.int32(t)) for t in range(1, UNITS)]
     for device in friends:
         pl.semaphore_signal(barrier, inc=1, device_id=device, device_id_type=MESH)
     load_g(1).start()
-    decode(0)
+    load_e.wait()
+
+    def begin(h, _):
+        y = h * yl + (1 - h) * (1 - yl)
+
+        @pl.when(h == 0)
+        def _():
+            load_half(1 - yl, 0).wait()
+
+        @pl.when(h == 1)
+        def _():
+            load_half(yl, UNITS // 2).wait()
+
+        decode_half(0, y)
+
+        @pl.when(h == 0)
+        def _():
+            pl.semaphore_wait(barrier, len(friends))
+            y1(jnp.int32(0))
+
+        return 0
+
+    lax.fori_loop(0, 2, begin, 0)
+    x1(jnp.int32(0))
     for p in range(2, UNITS // 2):
         load_g(p).start()
     for load in loads:
         load.start()
-    pl.semaphore_wait(barrier, len(friends))
 
     stages = dict(
         x1=x1, y1=y1, x2=x2, y2=y2, x3=x3, y3=y3, z4=z4, z5=z5, gx1=gx1, gy1=gy1, gx2=gx2, gy2=gy2, gx3=gx3, gy3=gy3
@@ -280,7 +312,7 @@
 
             else:
 
-                @pl.when((s >= lag) & (s < UNITS + lag))
+                @pl.when((s >= lag + (name[1] == "1")) & (s < UNITS + lag))
                 def _(lag=lag, stage=stages[name]):
                     stage(s - lag)
 
@@ -296,10 +328,13 @@
         remote(ref, ref, i, gx3_sem, right).wait_send()
 
 
-def order_kernel(layout, raw, mas, mom, out, new_master, new_momentum, staged, sems):
+def order_kernel(layout_far, raw, mas, mom, out, new_master, new_momentum, layout, staged, sems):
+    load = pltpu.make_async_copy(layout_far, layout, sems.at[10])
+    load.start()
     copies = [pltpu.make_async_copy(mas, new_master, sems.at[8]), pltpu.make_async_copy(mom, new_momentum, sems.at[9])]
     for copy in copies:
         copy.start()
+    load.wait()
     for s in range(8):
         l = layout[s]
 
@@ -329,10 +364,11 @@
             pltpu.VMEM(master.shape, F32),
             pltpu.VMEM(master.shape, F32),
         ),
-        in_specs=[far, near, far, far],
+        in_specs=[far, far, far, far],
         out_specs=(far, near, near),
         scratch_shapes=[
             pltpu.VMEM((UNITS // 2, 8, 128, 512), BF16),
+            pltpu.VMEM((4, 8192), jnp.int32),
             vmem(UNITS, 2, 4, TILES),
             vmem(UNITS, 2, XT),
             vmem(UNITS, 4, YT),
@@ -343,7 +379,8 @@
             vmem(UNITS, TILES),
             pltpu.VMEM(master.shape, F32),
             pltpu.VMEM(master.shape, F32),
-            dma(UNITS // 2),
+            dma(UNITS // 2 + 1),
+            pltpu.SemaphoreType.DMA,
             dma(2),
             pltpu.SemaphoreType.DMA,
             dma(4),
@@ -363,9 +400,9 @@
             jax.ShapeDtypeStruct(master.shape, F32),
             jax.ShapeDtypeStruct(master.shape, F32),
         ),
-        in_specs=[pl.BlockSpec(memory_space=pltpu.SMEM), near, near, near],
+        in_specs=[far, near, near, near],
         out_specs=(far, far, far),
-        scratch_shapes=[pltpu.VMEM((8, 1024, 512), BF16), dma(10)],
+        scratch_shapes=[pltpu.SMEM((8,), jnp.int32), pltpu.VMEM((8, 1024, 512), BF16), dma(11)],
         compiler_params=pltpu.CompilerParams(vmem_limit_bytes=12 * 2**20),
         name="layer_order",
     )(layout, *results)

time: 127 us -> 124 us (0.976)
  Pallas kernels: 126 us -> 123 us
    pallas_call x1, Pallas kernels: 121 us -> 118 us  [per_device(): pl.pallas_call(step_kernel, out_shape=(pltpu.VMEM((UNITS, 2, 4) + tiles,...]
where the time goes in v4:
time: 124 us; the launch traced here: 123 us
  Pallas kernels  123 us (99%)
    pallas_call x1, Pallas kernels, per_device(): pl.pallas_call(step_kernel, out_shape=(pltpu.VMEM((UNITS, 2, 4) + tiles,...  118 us
    pallas_call x1, Pallas kernels, per_device(): pl.pallas_call(order_kernel, out_shape=(jax.ShapeDtypeStruct((8192, 512),...  4.74 us

profile of v4, /device:TPU:0, one launch (start us, length us, event | category | flops | bytes accessed | tf_op | source)
XLA Modules:
  0.0 123.5 jit_solution(13076653315651330385)
XLA Ops:
  0.6 0.0 copy-start
  0.6 118.1 %sum_update_gather.1 = (bf16[16,2,4,16,16,128]{5,4,3,2,1,0:T(8,128)(2,1)S(1)}, f32[64,8192]{1,0:T(8,128)S(1)}, f32[64,8192]{1,0:T(8,128)S(1)}) custom-call(bf16[8,8,128,512]{3,2,1,0:T(8,128)(2,1)} %bitcast.4, s32[4,8192]{1,0:T(4,128)} %bitcast.5, f32[64,8192]{1,0:T(8,128)} %master.1, f32[64,8192]{1,0:T(8,128)} %momentum.1), custom_call_target="tpu_custom_call" | custom-call | tf_op jit(solution)/shard_map/sum_update_gather/pallas_call | solution.py:360
  118.7 0.0 copy-done
  118.7 4.7 %layer_order.1 = (bf16[8192,512]{1,0:T(8,128)(2,1)}, f32[64,8192]{1,0:T(8,128)}, f32[64,8192]{1,0:T(8,128)}) custom-call(s32[8]{0:T(128)S(1)} %copy-done, bf16[16,2,4,16,16,128]{5,4,3,2,1,0:T(8,128)(2,1)S(1)} %get-tuple-element.9.raw, f32[64,8192]{1,0:T(8,128)S(1)} %get-tuple-element.10.mas, f32[64,8192]{1,0:T(8,128)S(1)} %get-tuple-element.11.mom), custom_call_target="tpu_custom_call" | custom-call | tf_op jit(solution)/shard_map/layer_order/pallas_call | solution.py:396
Async XLA Ops:
  0.6 118.1 %copy-start = (s32[8]{0:T(128)S(1)}, s32[8]{0:T(128)}, u32[]{:S(2)}) copy-start(s32[8]{0:T(128)} %layout_far.1) | copy-start | bytes 100

commit v5 on v4

--- a/solution.py
+++ b/solution.py
@@ -21,7 +21,8 @@
 
 
 ORDER = (
-    ("x1", 0), ("y1", 0), ("decode", 0), ("x2", 3), ("y2", 4), ("x3", 6), ("y3", 6), ("z4", 9), ("z5", 11), ("gx1", 13), ("gy1", 13), ("gx2", 16), ("gy2", 15), ("gx3", 22), ("gy3", 17),
+    ("x1", 0), ("y1", 0), ("decode", 0), ("x2", 3), ("y2", 4), ("x3", 6), ("y3", 6), ("z4", 9), ("z5", 12),
+    ("gx1", 15), ("gy1", 15), ("gx2", 18), ("gy2", 17), ("gx3", 24), ("gy3", 19),
 )
 
 
@@ -44,12 +45,13 @@
     g, exps, master, momentum,
     isl, new_master, new_momentum,
     graw, expt, dec, r1x, r1y, r2x, r2y, r3, a2a, ret, mas, mom,
-    g_sem, e_sem, m_sem, own_sem, send_sem, x1_sem, y1_sem, x2_sem, y2_sem, r3_sem, a_sem, b_sem,
+    go_sem, g_sem, e_sem, m_sem, own_sem, send_sem, x1_sem, y1_sem, x2_sem, y2_sem, r3_sem, a_sem, b_sem,
     gx1_sem, gy1_sem, gx2_sem, gy2_sem, gx3_sem, gy3_sem,
 ):
     rep, fs = lax.axis_index("replica"), lax.axis_index("fsdp")
     x, yl = lax.rem(rep, 4), lax.div(rep, 4)
-    turn = 2 * lax.rem(fs, 2)
+    core = lax.rem(fs, 2)
+    turn = 2 * core
     xp, xm, xo = lax.rem(x + 1 + turn, 4), lax.rem(x + 3 + turn, 4), lax.rem(x + 2, 4)
     right, left, side = (yl * 4 + xp, fs), (yl * 4 + xm, fs), ((1 - yl) * 4 + x, fs)
     swaps = [(1 - 2 * bit(fs, b)) * (1 << b) for b in range(4)]
@@ -78,6 +80,7 @@
         return pltpu.make_async_copy(g.at[at, lax.div(fs, 2)], graw.at[0, at], g_sem.at[sem])
 
     load_e = pltpu.make_async_copy(exps, expt, e_sem)
+    barrier = pltpu.get_barrier_semaphore()
     loads = (
         pltpu.make_async_copy(master, mas, m_sem.at[0]),
         pltpu.make_async_copy(momentum, mom, m_sem.at[1]),
@@ -192,6 +195,15 @@
         def _():
             a2a[0] = dec[0, yl, x]
 
+            @pl.when(core == 1)
+            def _():
+                pl.semaphore_wait(barrier, 14)
+                pl.semaphore_signal(go_sem, inc=1, device_id=(rep, fs - 1), device_id_type=MESH)
+
+            @pl.when(core == 0)
+            def _():
+                pl.semaphore_wait(go_sem, 1)
+
     def z5(t):
         @pl.when(t > 0)
         def _():
@@ -261,13 +273,19 @@
         arrived(isl.at[j, o, xo, ty], gy2_sem.at[t])
         spread(isl.at[j, o, every, ty], gy3_sem, side)
 
-    barrier = pltpu.get_barrier_semaphore()
     load_e.start()
     load_half(1 - yl, 0).start()
     load_half(yl, UNITS // 2).start()
-    friends = [right, left, side] + [partner(jnp.int32(t)) for t in range(1, UNITS)]
-    for device in friends:
-        pl.semaphore_signal(barrier, inc=1, device_id=device, device_id_type=MESH)
+    for where, _ in (right, left, side):
+        pl.semaphore_signal(barrier, inc=1, device_id=(where, fs - core), device_id_type=MESH)
+    for t in range(2, UNITS, 2):
+        where, there = partner(jnp.int32(t))
+        pl.semaphore_signal(barrier, inc=1, device_id=(where, there - core + 1), device_id_type=MESH)
+
+    @pl.when(core == 1)
+    def _():
+        pl.semaphore_signal(barrier, inc=1, device_id=(rep, fs - 1), device_id_type=MESH)
+
     load_g(1).start()
     load_e.wait()
 
@@ -286,7 +304,15 @@
 
         @pl.when(h == 0)
         def _():
-            pl.semaphore_wait(barrier, len(friends))
+            @pl.when(core == 0)
+            def _():
+                pl.semaphore_wait(barrier, 7)
+                pl.semaphore_signal(go_sem, inc=1, device_id=(rep, fs + 1), device_id_type=MESH)
+
+            @pl.when(core == 1)
+            def _():
+                pl.semaphore_wait(go_sem, 1)
+
             y1(jnp.int32(0))
 
         return 0
@@ -379,6 +405,7 @@
             vmem(UNITS, TILES),
             pltpu.VMEM(master.shape, F32),
             pltpu.VMEM(master.shape, F32),
+            pltpu.SemaphoreType.REGULAR,
             dma(UNITS // 2 + 1),
             pltpu.SemaphoreType.DMA,
             dma(2),

time: 124 us -> 119 us (0.960)
  Pallas kernels: 123 us -> 118 us
    pallas_call x1, Pallas kernels: 118 us -> 114 us  [per_device(): pl.pallas_call(step_kernel, out_shape=(pltpu.VMEM((UNITS, 2, 4) + tiles,...]
where the time goes in v5:
time: 119 us
  Pallas kernels  118 us (99%)
    pallas_call x1, Pallas kernels, per_device(): pl.pallas_call(step_kernel, out_shape=(pltpu.VMEM((UNITS, 2, 4) + tiles,...  114 us
    pallas_call x1, Pallas kernels, per_device(): pl.pallas_call(order_kernel, out_shape=(jax.ShapeDtypeStruct((8192, 512),...  4.74 us

profile of v5, /device:TPU:0, one launch (start us, length us, event | category | flops | bytes accessed | tf_op | source)
XLA Modules:
  0.0 118.9 jit_solution(13389912553665006790)
XLA Ops:
  0.6 0.0 copy-start
  0.6 113.5 %sum_update_gather.1 = (bf16[16,2,4,16,16,128]{5,4,3,2,1,0:T(8,128)(2,1)S(1)}, f32[64,8192]{1,0:T(8,128)S(1)}, f32[64,8192]{1,0:T(8,128)S(1)}) custom-call(bf16[8,8,128,512]{3,2,1,0:T(8,128)(2,1)} %bitcast.4, s32[4,8192]{1,0:T(4,128)} %bitcast.5, f32[64,8192]{1,0:T(8,128)} %master.1, f32[64,8192]{1,0:T(8,128)} %momentum.1), custom_call_target="tpu_custom_call" | custom-call | tf_op jit(solution)/shard_map/sum_update_gather/pallas_call | solution.py:386
  114.2 0.0 copy-done
  114.2 4.7 %layer_order.1 = (bf16[8192,512]{1,0:T(8,128)(2,1)}, f32[64,8192]{1,0:T(8,128)}, f32[64,8192]{1,0:T(8,128)}) custom-call(s32[8]{0:T(128)S(1)} %copy-done, bf16[16,2,4,16,16,128]{5,4,3,2,1,0:T(8,128)(2,1)S(1)} %get-tuple-element.9.raw, f32[64,8192]{1,0:T(8,128)S(1)} %get-tuple-element.10.mas, f32[64,8192]{1,0:T(8,128)S(1)} %get-tuple-element.11.mom), custom_call_target="tpu_custom_call" | custom-call | tf_op jit(solution)/shard_map/layer_order/pallas_call | solution.py:423
Async XLA Ops:
  0.6 113.6 %copy-start = (s32[8]{0:T(128)S(1)}, s32[8]{0:T(128)}, u32[]{:S(2)}) copy-start(s32[8]{0:T(128)} %layout_far.1) | copy-start | bytes 100

commit v6 on v5

--- a/solution.py
+++ b/solution.py
@@ -18,6 +18,7 @@
 YT = TILES - XT
 YP = 3
 YM = XT + YP
+WINDOW = 8
 
 
 ORDER = (
@@ -139,48 +140,48 @@
         lax.fori_loop(0, 2, one, 0)
 
     def x1(t):
-        send(dec.at[t, every, xo, txp], r1x.at[t, every, txp], x1_sem.at[t], right)
-        send(dec.at[t, every, xo, txm], r1x.at[t, every, txm], x1_sem.at[t], left)
+        send(dec.at[t, every, xo, txp], r1x.at[t, every, txp], x1_sem.at[lax.rem(t, WINDOW)], right)
+        send(dec.at[t, every, xo, txm], r1x.at[t, every, txm], x1_sem.at[lax.rem(t, WINDOW)], left)
 
     def y1(t):
         send(dec.at[t, 1 - own(t), every, ty], r1y.at[t], y1_sem.at[t], side)
 
     def x2(t):
-        arrived(r1x.at[t], x1_sem.at[t])
+        arrived(r1x.at[t], x1_sem.at[lax.rem(t, WINDOW)])
         at = (t, every, xp, txp)
         dec[at] = (wide(dec, *at) + wide(r1x, t, every, txp)).astype(BF16)
-        send(dec.at[t, every, xp, tx], r2x.at[t, 0], x2_sem.at[t], right)
+        send(dec.at[t, every, xp, tx], r2x.at[t, 0], x2_sem.at[lax.rem(t, WINDOW)], right)
         at = (t, every, xm, txm)
         dec[at] = (wide(dec, *at) + wide(r1x, t, every, txm)).astype(BF16)
-        send(dec.at[t, every, xm, tx], r2x.at[t, 1], x2_sem.at[t], left)
+        send(dec.at[t, every, xm, tx], r2x.at[t, 1], x2_sem.at[lax.rem(t, WINDOW)], left)
 
     def y2(t):
         arrived(r1y.at[t], y1_sem.at[t])
         o = own(t)
         at = (t, o, every, ty)
         dec[at] = (wide(dec, *at) + wide(r1y, t)).astype(BF16)
-        send(dec.at[t, o, xo, typ], r2y.at[t, pl.ds(0, YP)], y2_sem.at[t], right)
-        send(dec.at[t, o, xo, tym], r2y.at[t, pl.ds(YP, YT - YP)], y2_sem.at[t], left)
+        send(dec.at[t, o, xo, typ], r2y.at[t, pl.ds(0, YP)], y2_sem.at[lax.rem(t, WINDOW)], right)
+        send(dec.at[t, o, xo, tym], r2y.at[t, pl.ds(YP, YT - YP)], y2_sem.at[lax.rem(t, WINDOW)], left)
 
     def x3(t):
-        arrived(r2x.at[t], x2_sem.at[t])
+        arrived(r2x.at[t], x2_sem.at[lax.rem(t, WINDOW)])
         o = 1 - own(t)
         at = (t, o, x, tx)
         dec[at] = (wide(dec, *at) + wide(r2x, t, 0, o) + wide(r2x, t, 1, o)).astype(BF16)
-        send(dec.at[at], r3.at[t, tx], r3_sem.at[t], side)
+        send(dec.at[at], r3.at[t, tx], r3_sem.at[lax.rem(t, WINDOW)], side)
 
     def y3(t):
-        arrived(r2y.at[t], y2_sem.at[t])
+        arrived(r2y.at[t], y2_sem.at[lax.rem(t, WINDOW)])
         o = own(t)
         at = (t, o, xp, typ)
         dec[at] = (wide(dec, *at) + wide(r2y, t, pl.ds(0, YP))).astype(BF16)
-        send(dec.at[t, o, xp, ty], r3.at[t, pl.ds(XT, YT)], r3_sem.at[t], right)
+        send(dec.at[t, o, xp, ty], r3.at[t, pl.ds(XT, YT)], r3_sem.at[lax.rem(t, WINDOW)], right)
         at = (t, o, xm, tym)
         dec[at] = (wide(dec, *at) + wide(r2y, t, pl.ds(YP, YT - YP))).astype(BF16)
-        send(dec.at[t, o, xm, ty], r3.at[t, pl.ds(XT + YT, YT)], r3_sem.at[t], left)
+        send(dec.at[t, o, xm, ty], r3.at[t, pl.ds(XT + YT, YT)], r3_sem.at[lax.rem(t, WINDOW)], left)
 
     def z4(t):
-        arrived(r3.at[t], r3_sem.at[t])
+        arrived(r3.at[t], r3_sem.at[lax.rem(t, WINDOW)])
         o = own(t)
         at = (t, o, x, tx)
         dec[at] = (wide(dec, *at) + wide(r2x, t, 0, o) + wide(r2x, t, 1, o) + wide(r3, t, tx)).astype(BF16)
@@ -242,25 +243,25 @@
 
     def gx1(t):
         ready(t)
-        spread(isl.at[other(t), own(t), x, tx], gx1_sem.at[t], side)
+        spread(isl.at[other(t), own(t), x, tx], gx1_sem.at[lax.rem(t, WINDOW)], side)
 
     def gy1(t):
         at = isl.at[other(t), own(t), x, ty]
-        spread(at, gy1_sem.at[t], right)
-        spread(at, gy1_sem.at[t], left)
+        spread(at, gy1_sem.at[lax.rem(t, WINDOW)], right)
+        spread(at, gy1_sem.at[lax.rem(t, WINDOW)], left)
 
     def gx2(t):
         j = other(t)
-        arrived(isl.at[j, 1 - own(t), x, tx], gx1_sem.at[t])
+        arrived(isl.at[j, 1 - own(t), x, tx], gx1_sem.at[lax.rem(t, WINDOW)])
         at = isl.at[j, every, x, tx]
         spread(at, gx2_sem.at[t], right)
         spread(at, gx2_sem.at[t], left)
 
     def gy2(t):
         j, o = other(t), own(t)
-        arrived(isl.at[j, every, x, ty], gy1_sem.at[t])
-        spread(isl.at[j, o, xm, typ], gy2_sem.at[t], right)
-        spread(isl.at[j, o, xp, tym], gy2_sem.at[t], left)
+        arrived(isl.at[j, every, x, ty], gy1_sem.at[lax.rem(t, WINDOW)])
+        spread(isl.at[j, o, xm, typ], gy2_sem.at[lax.rem(t, WINDOW)], right)
+        spread(isl.at[j, o, xp, tym], gy2_sem.at[lax.rem(t, WINDOW)], left)
 
     def gx3(t):
         j = other(t)
@@ -270,7 +271,7 @@
 
     def gy3(t):
         j, o = other(t), own(t)
-        arrived(isl.at[j, o, xo, ty], gy2_sem.at[t])
+        arrived(isl.at[j, o, xo, ty], gy2_sem.at[lax.rem(t, WINDOW)])
         spread(isl.at[j, o, every, ty], gy3_sem, side)
 
     load_e.start()
@@ -314,6 +315,7 @@
                 pl.semaphore_wait(go_sem, 1)
 
             y1(jnp.int32(0))
+            y1(jnp.int32(1))
 
         return 0
 
@@ -338,7 +340,7 @@
 
             else:
 
-                @pl.when((s >= lag + (name[1] == "1")) & (s < UNITS + lag))
+                @pl.when((s >= lag + {"x1": 1, "y1": 2}.get(name, 0)) & (s < UNITS + lag))
                 def _(lag=lag, stage=stages[name]):
                     stage(s - lag)
 
@@ -412,7 +414,12 @@
             pltpu.SemaphoreType.DMA,
             dma(4),
         ]
-        + [dma(UNITS)] * 11
+        + [dma(WINDOW), dma(UNITS)]
+        + [dma(WINDOW)] * 3
+        + [dma(UNITS)] * 2
+        + [dma(WINDOW)] * 2
+        + [dma(UNITS)]
+        + [dma(WINDOW)]
         + [pltpu.SemaphoreType.DMA] * 2,
         compiler_params=pltpu.CompilerParams(
             collective_id=0, has_side_effects=True, vmem_limit_bytes=48 * 2**20

time: 119 us -> 119 us (level)
  no operation moved by 1% of the time
where the time goes in v6:
time: 119 us; the launch traced here: 118 us
  Pallas kernels  118 us (99%)
    pallas_call x1, Pallas kernels, per_device(): pl.pallas_call(step_kernel, out_shape=(pltpu.VMEM((UNITS, 2, 4) + tiles,...  113 us
    pallas_call x1, Pallas kernels, per_device(): pl.pallas_call(order_kernel, out_shape=(jax.ShapeDtypeStruct((8192, 512),...  4.74 us

profile of v6, /device:TPU:0, one launch (start us, length us, event | category | flops | bytes accessed | tf_op | source)
XLA Modules:
  0.0 118.4 jit_solution(5915393094908584628)
XLA Ops:
  0.6 0.0 copy-start
  0.6 113.0 %sum_update_gather.1 = (bf16[16,2,4,16,16,128]{5,4,3,2,1,0:T(8,128)(2,1)S(1)}, f32[64,8192]{1,0:T(8,128)S(1)}, f32[64,8192]{1,0:T(8,128)S(1)}) custom-call(bf16[8,8,128,512]{3,2,1,0:T(8,128)(2,1)} %bitcast.4, s32[4,8192]{1,0:T(4,128)} %bitcast.5, f32[64,8192]{1,0:T(8,128)} %master.1, f32[64,8192]{1,0:T(8,128)} %momentum.1), custom_call_target="tpu_custom_call" | custom-call | tf_op jit(solution)/shard_map/sum_update_gather/pallas_call | solution.py:388
  113.7 0.0 copy-done
  113.7 4.7 %layer_order.1 = (bf16[8192,512]{1,0:T(8,128)(2,1)}, f32[64,8192]{1,0:T(8,128)}, f32[64,8192]{1,0:T(8,128)}) custom-call(s32[8]{0:T(128)S(1)} %copy-done, bf16[16,2,4,16,16,128]{5,4,3,2,1,0:T(8,128)(2,1)S(1)} %get-tuple-element.9.raw, f32[64,8192]{1,0:T(8,128)S(1)} %get-tuple-element.10.mas, f32[64,8192]{1,0:T(8,128)S(1)} %get-tuple-element.11.mom), custom_call_target="tpu_custom_call" | custom-call | tf_op jit(solution)/shard_map/layer_order/pallas_call | solution.py:430
Async XLA Ops:
  0.6 113.1 %copy-start = (s32[8]{0:T(128)S(1)}, s32[8]{0:T(128)}, u32[]{:S(2)}) copy-start(s32[8]{0:T(128)} %layout_far.1) | copy-start | bytes 100
